TPU v7x, 256 devices: a whole 4x4x8 slice. The times are simulated.
256 devices in a mesh: tm: 32 (over z_lo, x, core), gz: 8 (over z_hi, y).
Axes of the slice: x: 4, y: 4, z: 8 (z_hi: 2, z_lo: 4; z = z_hi * 4 + z_lo), core: 2. Of those that a mesh axis runs over, the one named last changes fastest.
Arguments:
- iterate: float32 [32, 128, 128, 256], P('tm', 'gz'), may hold values from -6 to 6
- initial: float32 [128, 128, 256], P('gz'), may hold values from -6 to 6
Outputs:
- updated: float32 [32, 128, 128, 256], P('tm', 'gz')
All inputs are finite; a program needn't handle non-finite values.
Results may differ from a plain program's by a relative error of at most 0.0013.
Values sent between devices are 32-bit elements; how exact they have to be, the bound alone decides.
A program may use at most 128 MiB of HBM per device.

v0:
```python
import math

import jax
import jax.numpy as jnp
from jax import lax
from jax.sharding import PartitionSpec as P

NX = 256
NY = 128
NZ = 128


TIME_STEP = 0.05
DIFFUSION = 200.0
ALPHA_WEIGHT = 0.05
STABILIZER = 2.0
PRECISE = lax.Precision.HIGHEST
FORMS = {0: "jk,kabc->jabc", 1: "jk,akbc->ajbc", 2: "jk,abkc->abjc", 3: "jk,abck->abcj"}


def from_behind(value, axis, by):
    count = lax.axis_size(axis)
    pairs = [(i, i + by) for i in range(count) if 0 <= i + by < count]
    return lax.ppermute(value, axis, pairs)


def extended(cells, sides, width):
    for axis, dim in sides:
        count = lax.axis_size(axis)
        head = lax.slice_in_dim(cells, 0, width, axis=dim)
        tail = lax.slice_in_dim(cells, cells.shape[dim] - width, cells.shape[dim], axis=dim)
        cells = jnp.concatenate(
            [
                lax.ppermute(tail, axis, [(i, (i + 1) % count) for i in range(count)]),
                cells,
                lax.ppermute(head, axis, [((i + 1) % count, i) for i in range(count)]),
            ],
            axis=dim,
        )
    return cells


def tables(length, direction):
    positions = jnp.arange(length, dtype=jnp.int32)
    angles = (positions[:, None] * positions[None, :] % length).astype(jnp.float32) * (
        2.0 * math.pi / length
    )
    return (jnp.cos(angles), direction * jnp.sin(angles))


def apply_table(matrix, values, dim_id):
    return jnp.einsum(FORMS[dim_id], matrix, values, precision=PRECISE)


def transform(spec_re, spec_im, dim_id, direction):
    cos_table, sin_table = tables(spec_re.shape[dim_id], direction)
    if spec_im is None:
        return (apply_table(cos_table, spec_re, dim_id), apply_table(sin_table, spec_re, dim_id))
    out_re = apply_table(cos_table, spec_re, dim_id) - apply_table(sin_table, spec_im, dim_id)
    out_im = apply_table(sin_table, spec_re, dim_id) + apply_table(cos_table, spec_im, dim_id)
    return (out_re, out_im)


def real_part(spec_re, spec_im, dim_id):
    cos_table, sin_table = tables(spec_re.shape[dim_id], 1.0)
    return apply_table(cos_table, spec_re, dim_id) - apply_table(sin_table, spec_im, dim_id)


def indices_along(length, dim_id, start):
    shape_list = [1, 1, 1, 1]
    shape_list[dim_id] = length
    return (start + jnp.arange(length, dtype=jnp.int32)).reshape(shape_list)


def symbol(positions, length):
    return 2.0 * jnp.cos(positions.astype(jnp.float32) * (2.0 * math.pi / length)) - 2.0


def divide(spec_re, spec_im, freq_rows, z_rows, y_rows, x_rows, window):
    root = ALPHA_WEIGHT ** (1.0 / window)
    angles = freq_rows.astype(jnp.float32) * (2.0 * math.pi / window)
    total = symbol(z_rows, NZ) + symbol(y_rows, NY) + symbol(x_rows, NX)
    den_re = 1.0 - root * jnp.cos(angles) + TIME_STEP * (STABILIZER - DIFFUSION * total)
    den_im = root * jnp.sin(angles)
    modulus = den_re * den_re + den_im * den_im
    return (
        (spec_re * den_re + spec_im * den_im) / modulus,
        (spec_im * den_re - spec_re * den_im) / modulus,
    )


def body(iterate, initial):
    window = lax.axis_size("tm")
    step_index = lax.axis_index("tm")
    slab_index = lax.axis_index("gz")
    earlier = from_behind(iterate, "tm", 1)
    earlier = jnp.where(step_index == 0, initial[None], earlier)
    padded = extended(iterate, (("gz", 1),), 1)
    laplace = padded[:, 2:] + padded[:, :-2] - 6.0 * iterate
    laplace = laplace + jnp.roll(iterate, 1, 2) + jnp.roll(iterate, -1, 2)
    laplace = laplace + jnp.roll(iterate, 1, 3) + jnp.roll(iterate, -1, 3)
    residual = (
        earlier
        - iterate
        + TIME_STEP * (DIFFUSION * laplace + iterate - iterate * iterate * iterate)
    )
    damping = jnp.power(jnp.float32(ALPHA_WEIGHT), step_index.astype(jnp.float32) / window)
    source = residual * damping
    y_count = iterate.shape[2]
    x_count = iterate.shape[3]
    gathered = lax.all_to_all(source, "tm", split_axis=2, concat_axis=0, tiled=True)
    spec_re, spec_im = transform(gathered, None, 0, -1.0)
    spec_re, spec_im = (
        lax.all_to_all(spec_re, "tm", split_axis=0, concat_axis=2, tiled=True),
        lax.all_to_all(spec_im, "tm", split_axis=0, concat_axis=2, tiled=True),
    )
    spec_re, spec_im = transform(spec_re, spec_im, 3, -1.0)
    spec_re, spec_im = transform(spec_re, spec_im, 2, -1.0)
    y_dev = y_count // lax.axis_size("gz")
    pen_re, pen_im = transform(
        lax.all_to_all(spec_re, "gz", split_axis=2, concat_axis=1, tiled=True),
        lax.all_to_all(spec_im, "gz", split_axis=2, concat_axis=1, tiled=True),
        1,
        -1.0,
    )
    pen_re, pen_im = divide(
        pen_re,
        pen_im,
        step_index,
        indices_along(pen_re.shape[1], 1, 0),
        indices_along(y_dev, 2, slab_index * y_dev),
        indices_along(x_count, 3, 0),
        window,
    )
    pen_re, pen_im = transform(pen_re, pen_im, 1, 1.0)
    spec_re = lax.all_to_all(pen_re, "gz", split_axis=1, concat_axis=2, tiled=True)
    spec_im = lax.all_to_all(pen_im, "gz", split_axis=1, concat_axis=2, tiled=True)
    spec_re, spec_im = transform(spec_re, spec_im, 2, 1.0)
    spec_re, spec_im = transform(spec_re, spec_im, 3, 1.0)
    spec_re, spec_im = (
        lax.all_to_all(spec_re, "tm", split_axis=2, concat_axis=0, tiled=True),
        lax.all_to_all(spec_im, "tm", split_axis=2, concat_axis=0, tiled=True),
    )
    update = real_part(spec_re, spec_im, 0)
    update = lax.all_to_all(update, "tm", split_axis=0, concat_axis=2, tiled=True)
    update = update / (window * NZ * NY * NX)
    return iterate + update / damping


def solution(mesh):
    return jax.shard_map(
        body,
        mesh=mesh,
        in_specs=(P("tm", "gz", None, None), P("gz", None, None)),
        out_specs=P("tm", "gz", None, None),
        check_vma=False,
    )
```

profile of v0, /device:TPU:1, one launch (start us, length us, event | category | flops | bytes accessed | tf_op | source)
XLA Modules:
  0.0 667.7 jit_solution(5312266814070226861)
XLA Ops:
  2.8 4.5 collective-permute-start
  8.5 9.4 %collective-permute-start.1 = (f32[1,1,128,256]{3,1,0,2:T(1,128)S(1)}, f32[1,1,128,256]{3,1,0,2:T(1,128)S(1)}, u32[]{:S(2)}, u32[]{:S(2)}) collective-permute-start(f32[1,1,128,256]{3,1,0,2:T(1,128)S(1)} %copy.137), channel_id=1, source_target_pairs={{1,0},{2,1},{3,2},{4,3},{5,4},{6,5},{7,6},{0,7},{9,8},{10,9},{11,1... | collective-permute-start | bytes 393224 | tf_op jit(solution)/shard_map/ppermute | solution.py:36
  23.5 8.1 %collective-permute-done.2 = f32[1,1,128,256]{3,1,0,2:T(1,128)S(1)} collective-permute-done((f32[1,1,128,256]{3,1,0,2:T(1,128)S(1)}, f32[1,1,128,256]{3,1,0,2:T(1,128)S(1)}, u32[]{:S(2)}, u32[]{:S(2)}) %collective-permute-start.2) | collective-permute-done | bytes 131104 | tf_op jit(solution)/shard_map/ppermute | solution.py:34
  31.6 5.7 fusion.3
  37.3 67.6 %all_to_all.153 = f32[1,16,128,256]{3,1,0,2:T(8,128)S(1)} all-to-all(f32[1,16,128,256]{3,1,0,2:T(8,128)S(1)} %fusion.3), channel_id=1, replica_groups=mesh['tm'=32,'gz'=8] {'tm'}, dimensions={2} | all-to-all | bytes 4194304 | tf_op jit(solution)/shard_map/all_to_all | solution.py:111
  110.9 5.5 all-to-all-start.2
  122.5 42.2 %all-to-all-done.2 = f32[32,16,4,256]{3,2,1,0:T(4,128)} async-done(((f32[32,16,4,256]{3,2,1,0:T(4,128)}), f32[32,16,4,256]{3,2,1,0:T(4,128)}, u32[]{:S(2)}, u32[]{:S(2)}) %all-to-all-start.2) | async-done | bytes 2097184 | tf_op jit(solution)/shard_map/all_to_all | solution.py:115
  164.6 6.3 all-to-all-start.1
  173.0 5.1 fusion.41
  178.1 5.1 fusion.43
  183.2 35.9 %all-to-all-done.1 = f32[32,16,4,256]{3,2,1,0:T(4,128)S(1)} async-done(((f32[32,16,4,256]{3,2,1,0:T(4,128)}), f32[32,16,4,256]{3,2,1,0:T(4,128)S(1)}, u32[]{:S(2)}, u32[]{:S(2)}) %all-to-all-start.1) | async-done | bytes 2097184 | tf_op jit(solution)/shard_map/all_to_all | solution.py:114
  220.7 12.6 %fusion.57 = f32[16,128,256]{2,1,0:T(8,128)S(1)} fusion(f32[16,128,256]{2,1,0:T(8,128)S(1)} %copy-done.10, f32[16,128,256]{2,0,1:T(8,128)S(1)} %bitcast.235), kind=kOutput, calls=%fused_computation.71 | convolution fusion | flops 1612120064 | bytes 6291456 | tf_op jit(solution)/shard_map/jk,abck->abcj/dot_general | solution.py:52
  240.9 5.1 subtract_bitcast_fusion.2
  253.5 5.2 fusion.110
  258.8 4.9 add_bitcast_fusion.2
  266.7 16.3 %all-to-all-done.3 = f32[1,16,128,256]{3,1,0,2:T(8,128)} async-done(((f32[1,16,128,256]{3,1,0,2:T(8,128)}), f32[1,16,128,256]{3,1,0,2:T(8,128)}, u32[]{:S(2)}, u32[]{:S(2)}) %all-to-all-start.3) | async-done | bytes 2097184 | tf_op jit(solution)/shard_map/all_to_all | solution.py:121
  283.0 6.6 all-to-all-start.4
  303.1 17.6 %all-to-all-done.4 = f32[1,16,128,256]{3,1,0,2:T(8,128)} async-done(((f32[1,16,128,256]{3,1,0,2:T(8,128)}), f32[1,16,128,256]{3,1,0,2:T(8,128)}, u32[]{:S(2)}, u32[]{:S(2)}) %all-to-all-start.4) | async-done | bytes 2097184 | tf_op jit(solution)/shard_map/all_to_all | solution.py:122
  343.4 9.3 %all-to-all-start.5 = ((f32[1,128,16,256]{3,2,0,1:T(8,128)}), f32[1,128,16,256]{3,2,0,1:T(8,128)}, u32[]{:S(2)}, u32[]{:S(2)}) async-start(f32[1,128,16,256]{3,2,0,1:T(8,128)} %copy.177), calls=%async_computation.5 | async-start | bytes 4194304 | tf_op jit(solution)/shard_map/all_to_all | solution.py:136
  359.7 11.4 %all-to-all-done.5 = f32[1,128,16,256]{3,2,0,1:T(8,128)} async-done(((f32[1,128,16,256]{3,2,0,1:T(8,128)}), f32[1,128,16,256]{3,2,0,1:T(8,128)}, u32[]{:S(2)}, u32[]{:S(2)}) %all-to-all-start.5) | async-done | bytes 2097184 | tf_op jit(solution)/shard_map/all_to_all | solution.py:136
  377.3 5.0 fusion.115
  382.3 5.0 fusion.101
  387.3 12.2 %all-to-all-done.6 = f32[1,128,16,256]{3,2,0,1:T(8,128)S(1)} async-done(((f32[1,128,16,256]{3,2,0,1:T(8,128)}), f32[1,128,16,256]{3,2,0,1:T(8,128)S(1)}, u32[]{:S(2)}, u32[]{:S(2)}) %all-to-all-start.6) | async-done | bytes 2097184 | tf_op jit(solution)/shard_map/all_to_all | solution.py:137
  408.4 4.5 fusion.16
  420.1 77.5 %all-to-all-start.8 = ((f32[1,16,128,256]{3,1,0,2:T(8,128)}), f32[1,16,128,256]{3,1,0,2:T(8,128)}, u32[]{:S(2)}, u32[]{:S(2)}) async-start(f32[1,16,128,256]{3,1,0,2:T(8,128)} %copy.191), calls=%async_computation.8 | async-start | bytes 4194304 | tf_op jit(solution)/shard_map/all_to_all | solution.py:142
  497.7 6.0 fusion.18
  510.6 35.3 %all-to-all-done.8 = f32[1,16,128,256]{3,1,0,2:T(8,128)} async-done(((f32[1,16,128,256]{3,1,0,2:T(8,128)}), f32[1,16,128,256]{3,1,0,2:T(8,128)}, u32[]{:S(2)}, u32[]{:S(2)}) %all-to-all-start.8) | async-done | bytes 2097184 | tf_op jit(solution)/shard_map/all_to_all | solution.py:142
  545.9 6.3 all-to-all-start.7
  552.2 6.0 fusion.12
  558.2 42.1 %all-to-all-done.7 = f32[1,16,128,256]{3,1,0,2:T(8,128)S(1)} async-done(((f32[1,16,128,256]{3,1,0,2:T(8,128)}), f32[1,16,128,256]{3,1,0,2:T(8,128)S(1)}, u32[]{:S(2)}, u32[]{:S(2)}) %all-to-all-start.7) | async-done | bytes 2097184 | tf_op jit(solution)/shard_map/all_to_all | solution.py:141
  600.4 4.9 fusion.51
  606.7 55.2 %all_to_all.154 = f32[32,16,4,256]{3,2,1,0:T(4,128)S(1)} all-to-all(f32[32,16,4,256]{3,2,1,0:T(4,128)S(1)} %copy.193), channel_id=1, replica_groups=mesh['tm'=32,'gz'=8] {'tm'}, dimensions={0} | all-to-all | bytes 4194304 | tf_op jit(solution)/shard_map/all_to_all | solution.py:145
  (82 shorter events, 122.0 us)
Async XLA Ops:
  2.8 28.8 %collective-permute-start = (f32[1,16,128,256]{3,1,0,2:T(8,128)S(1)}, f32[1,16,128,256]{3,1,0,2:T(8,128)}, u32[]{:S(2)}, u32[]{:S(2)}) collective-permute-start(f32[1,16,128,256]{3,1,0,2:T(8,128)S(1)} %copy.135), channel_id=1, source_target_pairs={{0,8},{8,16},{16,24},{24,32},{32,40},{40,48},{48,56},{56,64},{64,7... | collective-permute-start | bytes 6291464 | tf_op jit(solution)/shard_map/ppermute | solution.py:24
  8.5 15.0 %collective-permute-start.1 = (f32[1,1,128,256]{3,1,0,2:T(1,128)S(1)}, f32[1,1,128,256]{3,1,0,2:T(1,128)S(1)}, u32[]{:S(2)}, u32[]{:S(2)}) collective-permute-start(f32[1,1,128,256]{3,1,0,2:T(1,128)S(1)} %copy.137), channel_id=1, source_target_pairs={{1,0},{2,1},{3,2},{4,3},{5,4},{6,5},{7,6},{0,7},{9,8},{10,9},{11,1... | collective-permute-start | bytes 393224 | tf_op jit(solution)/shard_map/ppermute | solution.py:36
  18.0 13.5 %collective-permute-start.2 = (f32[1,1,128,256]{3,1,0,2:T(1,128)S(1)}, f32[1,1,128,256]{3,1,0,2:T(1,128)S(1)}, u32[]{:S(2)}, u32[]{:S(2)}) collective-permute-start(f32[1,1,128,256]{3,1,0,2:T(1,128)S(1)} %copy.139), channel_id=1, source_target_pairs={{0,1},{1,2},{2,3},{3,4},{4,5},{5,6},{6,7},{7,0},{8,9},{9,10},{10,1... | collective-permute-start | bytes 393224 | tf_op jit(solution)/shard_map/ppermute | solution.py:34
  19.1 12.5 %copy-start.12 = (f32[16,128,256]{2,1,0:T(8,128)S(1)}, f32[16,128,256]{2,1,0:T(8,128)}, u32[]{:S(2)}) copy-start(f32[16,128,256]{2,1,0:T(8,128)} %param.3) | copy-start | bytes 6291460
  110.9 53.7 %all-to-all-start.2 = ((f32[32,16,4,256]{3,2,1,0:T(4,128)}), f32[32,16,4,256]{3,2,1,0:T(4,128)}, u32[]{:S(2)}, u32[]{:S(2)}) async-start(f32[32,16,4,256]{3,2,1,0:T(4,128)} %copy.158), calls=%async_computation.2 | async-start | bytes 4194304 | tf_op jit(solution)/shard_map/all_to_all | solution.py:115
  164.6 54.5 %all-to-all-start.1 = ((f32[32,16,4,256]{3,2,1,0:T(4,128)}), f32[32,16,4,256]{3,2,1,0:T(4,128)S(1)}, u32[]{:S(2)}, u32[]{:S(2)}) async-start(f32[32,16,4,256]{3,2,1,0:T(4,128)} %copy.155), calls=%async_computation.1 | async-start | bytes 4194304 | tf_op jit(solution)/shard_map/all_to_all | solution.py:114
  219.1 1.6 copy-start.10
  220.7 12.7 %copy-start.8 = (f32[16,128,256]{2,1,0:T(8,128)S(1)}, f32[16,128,256]{2,1,0:T(8,128)}, u32[]{:S(2)}) copy-start(f32[16,128,256]{2,1,0:T(8,128)} %fusion.43) | copy-start | bytes 6291460
  237.3 3.6 copy-start
  249.2 33.8 %all-to-all-start.3 = ((f32[1,16,128,256]{3,1,0,2:T(8,128)}), f32[1,16,128,256]{3,1,0,2:T(8,128)}, u32[]{:S(2)}, u32[]{:S(2)}) async-start(f32[1,16,128,256]{3,1,0,2:T(8,128)} %copy.165), calls=%async_computation.3 | async-start | bytes 4194304 | tf_op jit(solution)/shard_map/all_to_all | solution.py:121
  283.0 37.6 %all-to-all-start.4 = ((f32[1,16,128,256]{3,1,0,2:T(8,128)}), f32[1,16,128,256]{3,1,0,2:T(8,128)}, u32[]{:S(2)}, u32[]{:S(2)}) async-start(f32[1,16,128,256]{3,1,0,2:T(8,128)} %copy.171), calls=%async_computation.4 | async-start | bytes 4194304 | tf_op jit(solution)/shard_map/all_to_all | solution.py:122
  327.1 3.9 copy-start.7
  331.1 5.2 copy-start.3
  333.3 3.0 copy-start.5
  343.4 27.8 %all-to-all-start.5 = ((f32[1,128,16,256]{3,2,0,1:T(8,128)}), f32[1,128,16,256]{3,2,0,1:T(8,128)}, u32[]{:S(2)}, u32[]{:S(2)}) async-start(f32[1,128,16,256]{3,2,0,1:T(8,128)} %copy.177), calls=%async_computation.5 | async-start | bytes 4194304 | tf_op jit(solution)/shard_map/all_to_all | solution.py:136
  352.7 2.1 copy-start.4
  352.7 2.2 copy-start.6
  371.2 28.3 %all-to-all-start.6 = ((f32[1,128,16,256]{3,2,0,1:T(8,128)}), f32[1,128,16,256]{3,2,0,1:T(8,128)S(1)}, u32[]{:S(2)}, u32[]{:S(2)}) async-start(f32[1,128,16,256]{3,2,0,1:T(8,128)} %copy.180), calls=%async_computation.6 | async-start | bytes 4194304 | tf_op jit(solution)/shard_map/all_to_all | solution.py:137
  399.4 1.6 copy-start.11
  401.0 3.6 copy-start.9
  408.4 4.5 copy-start.1
  420.1 125.8 %all-to-all-start.8 = ((f32[1,16,128,256]{3,1,0,2:T(8,128)}), f32[1,16,128,256]{3,1,0,2:T(8,128)}, u32[]{:S(2)}, u32[]{:S(2)}) async-start(f32[1,16,128,256]{3,1,0,2:T(8,128)} %copy.191), calls=%async_computation.8 | async-start | bytes 4194304 | tf_op jit(solution)/shard_map/all_to_all | solution.py:142
  545.9 54.4 %all-to-all-start.7 = ((f32[1,16,128,256]{3,1,0,2:T(8,128)}), f32[1,16,128,256]{3,1,0,2:T(8,128)S(1)}, u32[]{:S(2)}, u32[]{:S(2)}) async-start(f32[1,16,128,256]{3,1,0,2:T(8,128)} %copy.187), calls=%async_computation.7 | async-start | bytes 4194304 | tf_op jit(solution)/shard_map/all_to_all | solution.py:141
  661.9 1.6 copy-start.2
where the time goes:
time: 677 us; the launch traced here: 668 us
  waiting for transfers between devices  225 us (33%)
  starting transfers between devices  134 us (20%)
  matrix products  124 us (18%)
  blocking collectives  123 us (18%)
  local copies, waits for them, and re-layouts  52.6 us (8%)
  other arithmetic  8.51 us (1%)
    dot_general x28, matrix products, apply_table(): return jnp.einsum(FORMS[dim_id], matrix, values, precision=PRECISE)  124 us
    all_to_all x1, starting transfers between devices, body(): lax.all_to_all(spec_im, 'tm', split_axis=2, concat_axis=0, tiled=True)  77.5 us
    all_to_all x1, blocking collectives, body(): lax.all_to_all(source, 'tm', split_axis=2, concat_axis=0, tiled=True)  67.6 us
    all_to_all x1, blocking collectives, body(): lax.all_to_all(update, 'tm', split_axis=0, concat_axis=2, tiled=True)  55.2 us
    all_to_all x1, waiting for transfers between devices, body(): lax.all_to_all(spec_im, 'tm', split_axis=0, concat_axis=2, tiled=True)  42.2 us
    all_to_all x1, waiting for transfers between devices, body(): lax.all_to_all(spec_re, 'tm', split_axis=2, concat_axis=0, tiled=True)  42.1 us
    all_to_all x1, waiting for transfers between devices, body(): lax.all_to_all(spec_re, 'tm', split_axis=0, concat_axis=2, tiled=True)  35.9 us
    all_to_all x1, waiting for transfers between devices, body(): lax.all_to_all(spec_im, 'tm', split_axis=2, concat_axis=0, tiled=True)  35.3 us
  transfers between devices with their start and end apart: 11, of which 10 were waited for; matrix products, arithmetic and copies ran while one was open for 13% of the time, Pallas kernels for 0%

commit v1 on v0

v1 whole, which is shorter than its diff:
```python
import functools
import math

import jax
import jax.numpy as jnp
import ml_dtypes
import numpy as np
from jax import lax
from jax.experimental import pallas as pl
from jax.experimental.pallas import tpu as pltpu
from jax.sharding import PartitionSpec as P

MESH = pl.DeviceIdType.MESH
F32 = jnp.float32
BF16 = jnp.bfloat16

NX, NY, NZ, L = 256, 128, 128, 32
TIME_STEP, DIFFUSION, ALPHA, STABILIZER = 0.05, 200.0, 0.05, 2.0
COUPLING = TIME_STEP * DIFFUSION
BLOCK = 8
SLABS = 4
HALF = NZ // 2
PLANES = 16
ROWS = 4
SETS = 2
KS = ROWS // SETS
ZROWS = 16


def real_basis(n):
    pos = np.arange(n)
    rows, freq = [np.ones(n) / math.sqrt(n), np.cos(math.pi * pos) / math.sqrt(n)], [0, n // 2]
    for m in range(1, n // 2):
        rows += [np.cos(2 * math.pi * m * pos / n) * math.sqrt(2 / n)]
        rows += [np.sin(2 * math.pi * m * pos / n) * math.sqrt(2 / n)]
        freq += [m, m]
    return np.stack(rows), 2.0 - 2.0 * np.cos(2 * math.pi * np.array(freq) / n)


def parts(m):
    m = np.asarray(m, np.float32)
    hi = m.astype(ml_dtypes.bfloat16)
    return hi, (m - hi.astype(np.float32)).astype(ml_dtypes.bfloat16)


def left(m):
    hi, lo = parts(m)
    return np.concatenate([hi, lo, hi], axis=1)


def right(m):
    hi, lo = parts(m)
    return np.concatenate([hi, lo, hi], axis=0)


def wide(column):
    return np.broadcast_to(np.asarray(column, np.float32)[:, None], (len(column), 128)).copy()


def tables():
    bx, lx = real_basis(NX)
    by, ly = real_basis(NY)
    bz, lz = real_basis(NZ)
    k = np.arange(1, HALF + 1)
    sine = np.sin(math.pi * np.outer(k, k) / (HALF + 1)) * math.sqrt(2 / (HALF + 1))
    lk = 2.0 - 2.0 * np.cos(math.pi * k / (HALF + 1))
    sign = np.where((np.arange(NZ) // 2) % 2 == 0, 1.0, -1.0)
    base = 1.0 + TIME_STEP * STABILIZER
    return dict(
        bx_f=right(bx.T),
        by_f=left(by),
        bx_i=right(bx),
        by_i=left(by.T),
        bz_s=left(np.concatenate([bz[:, :HALF], sine], axis=0)),
        bz_f=left(bz[:, :HALF]),
        bz_i=left(sine @ bz[:, :HALF].T),
        sine=left(sine),
        lxy=(base + COUPLING * (ly[:, None] + lx[None, :])).astype(np.float32),
        lz=wide(COUPLING * lz),
        lk=wide(COUPLING * lk),
        sign=wide(sign),
        edges=np.stack([wide(bz[:, p]) for p in (HALF - 1, 0, NZ - 1, HALF)]),
        walls=np.stack([wide(COUPLING * sine[:, 0]), wide(COUPLING * sine[:, HALF - 1])]),
    )


TABLES = tables()
NAMES = sorted(TABLES)


def split(x):
    hi = x.astype(BF16)
    return hi, (x - hi.astype(F32)).astype(BF16)


def dot(a, b):
    return jnp.dot(a, b, preferred_element_type=F32)


def dot_left(table, x):
    hi, lo = split(x)
    return dot(table, jnp.concatenate([hi, hi, lo], axis=0))


def dot_right(x, table):
    hi, lo = split(x)
    return dot(jnp.concatenate([hi, hi, lo], axis=1), table)


def twice(x):
    return jnp.concatenate([x, x], axis=1)


def drain(ref, sem):
    pltpu.make_async_copy(ref, ref, sem).wait()


def kernel(u_ref, init_ref, *refs):
    tab = dict(zip(NAMES, refs[: len(NAMES)]))
    (out_ref, u, s, sp, r, pb, sq, ys, yr, es, ec, er, fs, p, ws, s2,
     usem, isem, bsend, brecv, psend, precv, dsend, drecv, esend, erecv, fsend, frecv, hsend, hrecv) = refs[len(NAMES):]
    tm, gz = lax.axis_index("tm"), lax.axis_index("gz")
    block, step = tm // BLOCK, tm % BLOCK
    half, slab = gz // SLABS, gz % SLABS
    place = step * SLABS + slab
    ring = block * 2 + half

    load = pltpu.make_async_copy(u_ref.at[0], u, usem)
    load.start()

    def plane_peer(i):
        t, y = (step + i % BLOCK) % BLOCK, (slab + i // BLOCK) % SLABS
        return t, y, (block * BLOCK + t, half * SLABS + y)

    def ring_peer(i):
        to_b, to_h = (block + i % 4) % 4, (half + i // 4) % 2
        return to_b, to_h, (to_b * BLOCK + step, to_h * SLABS + slab)

    barrier = pltpu.get_barrier_semaphore()

    def greet_plane(i, c):
        pl.semaphore_signal(barrier, inc=1, device_id=plane_peer(i)[2], device_id_type=MESH)
        return c

    def greet_ring(i, c):
        pl.semaphore_signal(barrier, inc=1, device_id=ring_peer(i)[2], device_id_type=MESH)
        return c

    lax.fori_loop(1, 32, greet_plane, 0)
    lax.fori_loop(1, 8, greet_ring, 0)
    load.wait()

    def forward(x, dst, z):
        rows = dot_right(x.reshape(4 * NY, NX), tab["bx_f"][...])
        for i in range(4):
            dst[:, z + i, :] = dot_left(tab["by_f"][...], rows[i * NY:(i + 1) * NY])

    for g in range(PLANES // 4):
        x = u[4 * g:4 * g + 4]
        forward(x * (TIME_STEP * (STABILIZER + 1.0) - TIME_STEP * x * x), s, 4 * g)
    pl.semaphore_wait(barrier, 38)

    def send_b(i, c, k):
        t, y, dev = plane_peer(i)
        pltpu.make_async_remote_copy(
            src_ref=s.at[pl.ds((t * SLABS + y) * ROWS + k * KS, KS)],
            dst_ref=r.at[k, step, :, pl.ds(pl.multiple_of(slab * PLANES, PLANES), PLANES), :],
            send_sem=bsend.at[k], recv_sem=brecv.at[k], device_id=dev, device_id_type=MESH,
        ).start()
        return c

    for k in range(SETS):
        lax.fori_loop(1, 32, functools.partial(send_b, k=k), 0)
        pltpu.make_async_copy(
            s.at[pl.ds(place * ROWS + k * KS, KS)],
            r.at[k, step, :, pl.ds(pl.multiple_of(slab * PLANES, PLANES), PLANES), :],
            brecv.at[k],
        ).start()

    @pl.when(tm == L - 1)
    def _():
        load2 = pltpu.make_async_copy(init_ref, out_ref.at[0], isem)
        load2.start()
        load2.wait()
        for g in range(PLANES // 4):
            forward(out_ref[0, 4 * g:4 * g + 4] * (1.0 / ALPHA) - u[4 * g:4 * g + 4], sp, 4 * g)

        def send_p(i, c):
            t, y, dev = plane_peer(i)
            pltpu.make_async_remote_copy(
                src_ref=sp.at[pl.ds((t * SLABS + y) * ROWS, ROWS)],
                dst_ref=pb.at[:, pl.ds(pl.multiple_of(slab * PLANES, PLANES), PLANES), :],
                send_sem=psend, recv_sem=precv, device_id=dev, device_id_type=MESH,
            ).start()
            return c

        lax.fori_loop(1, 32, send_p, 0)
        pltpu.make_async_copy(
            sp.at[pl.ds(place * ROWS, ROWS)],
            pb.at[:, pl.ds(pl.multiple_of(slab * PLANES, PLANES), PLANES), :],
            precv,
        ).start()

    def decay(k, j, table):
        row = tab["lxy"][pl.ds(place * ROWS + k * KS + j, 1), :]
        return 1.0 / (row + twice(table))

    def stage_c(k):
        drain(r.at[k], brecv.at[k])
        if k == 0:
            @pl.when(block == 3)
            def _():
                drain(pb, precv)

        def one(j, c):
            a = decay(k, j, tab["lz"][...])
            z = None
            edges = [twice(tab["edges"][e]) for e in range(4)]
            for t in range(BLOCK):
                both = dot_left(tab["bz_s"][...], r[k, t, j])
                sq[k, t, j] = both[NZ:]
                z = a * both[:NZ] if z is None else a * (both[:NZ] + z)
                for e in range(4):
                    row = jnp.sum(z * edges[e], axis=0, keepdims=True)
                    if e < 2:
                        es[k, j, pl.ds(2 * t + e, 1), :] = row
                    else:
                        ec[k, j, pl.ds(2 * t + e - 2, 1), :] = row
            ys[k, j] = z
            return c

        lax.fori_loop(0, KS, one, 0)

        @pl.when(block == 3)
        def _():
            def add(j, c):
                ys[k, j] += dot_left(tab["bz_f"][...], pb[k * KS + j])
                return c
            lax.fori_loop(0, KS, add, 0)

        def send_d(i, c):
            to_b, to_h, dev = ring_peer(i)
            pltpu.make_async_remote_copy(
                src_ref=ys.at[k, :, pl.ds(pl.multiple_of((to_b * 2 + to_h) * ZROWS, ZROWS), ZROWS), :],
                dst_ref=yr.at[k, ring],
                send_sem=dsend.at[k], recv_sem=drecv.at[k], device_id=dev, device_id_type=MESH,
            ).start()
            return c

        lax.fori_loop(1, 8, send_d, 0)
        pltpu.make_async_copy(
            ys.at[k, :, pl.ds(pl.multiple_of(ring * ZROWS, ZROWS), ZROWS), :], yr.at[k, ring], drecv.at[k]
        ).start()
        pltpu.make_async_remote_copy(
            src_ref=es.at[k], dst_ref=er.at[k], send_sem=esend.at[k], recv_sem=erecv.at[k],
            device_id=ring_peer(4)[2], device_id_type=MESH,
        ).start()

    def stage_e(k):
        drain(yr.at[k], drecv.at[k])
        lz = tab["lz"][pl.ds(pl.multiple_of(ring * ZROWS, ZROWS), ZROWS), :]
        sign = twice(tab["sign"][0:ZROWS])
        for j in range(KS):
            a = decay(k, j, lz)
            g = a * a
            g = g * g
            g = g * g
            ends = [yr[k, 2 * b, j] + sign * yr[k, 2 * b + 1, j] for b in range(4)]
            total = ends[0]
            for b in range(1, 4):
                total = ends[b] + g * total
            g4 = g * g
            g4 = g4 * g4
            prev = total * (ALPHA / (1.0 - ALPHA * g4))
            for b in range(4):
                fs[k, b, j] = prev
                prev = ends[b] + g * prev

        def send_f(i, c):
            to_b, to_h, dev = ring_peer(i)
            pltpu.make_async_remote_copy(
                src_ref=fs.at[k, to_b],
                dst_ref=p.at[k, :, pl.ds(pl.multiple_of(ring * ZROWS, ZROWS), ZROWS), :],
                send_sem=fsend.at[k], recv_sem=frecv.at[k], device_id=dev, device_id_type=MESH,
            ).start()
            return c

        lax.fori_loop(1, 8, send_f, 0)
        pltpu.make_async_copy(
            fs.at[k, block], p.at[k, :, pl.ds(pl.multiple_of(ring * ZROWS, ZROWS), ZROWS), :], frecv.at[k]
        ).start()

    def stage_g(k):
        drain(p.at[k], frecv.at[k])
        drain(er.at[k], erecv.at[k])
        mirrored = half.astype(F32)

        def one(j, c):
            a = decay(k, j, tab["lz"][...])
            ak = decay(k, j, tab["lk"][...])
            v = p[k, j] * twice(1.0 + mirrored * (tab["sign"][...] - 1.0))
            w = dot_left(tab["bz_i"][...], v)
            outer = [twice(tab["edges"][e]) for e in (2, 3)]
            walls = [twice(tab["walls"][e]) for e in range(2)]
            for t in range(BLOCK):
                v = v * a
                rhs = sq[k, t, j] + w
                for e in range(2):
                    row = jnp.sum(v * outer[e], axis=0, keepdims=True)
                    row = row + er[k, j, pl.ds(2 * t + e, 1), :] + ec[k, j, pl.ds(2 * t + e, 1), :]
                    rhs = rhs + walls[e] * row
                w = ak * rhs
                ws[k, t, j] = dot_left(tab["sine"][...], w)
            return c

        lax.fori_loop(0, KS, one, 0)

        def send_h(i, c):
            t, y, dev = plane_peer(i)
            pltpu.make_async_remote_copy(
                src_ref=ws.at[k, t, :, pl.ds(pl.multiple_of(y * PLANES, PLANES), PLANES), :],
                dst_ref=s2.at[pl.ds(place * ROWS + k * KS, KS)],
                send_sem=hsend, recv_sem=hrecv, device_id=dev, device_id_type=MESH,
            ).start()
            return c

        lax.fori_loop(1, 32, send_h, 0)
        pltpu.make_async_copy(
            ws.at[k, step, :, pl.ds(pl.multiple_of(slab * PLANES, PLANES), PLANES), :],
            s2.at[pl.ds(place * ROWS + k * KS, KS)],
            hrecv,
        ).start()

    if SETS == 1:
        order = [(stage_c, 0), (stage_e, 0), (stage_g, 0)]
    else:
        order = [(stage_c, 0), (stage_e, 0), (stage_c, 1), (stage_g, 0), (stage_e, 1), (stage_g, 1)]
    for stage, k in order:
        stage(k)

    drain(s2, hrecv)
    for g in range(PLANES // 4):
        cols = [dot_left(tab["by_i"][...], s2[:, 4 * g + i, :]) for i in range(4)]
        rows = dot_right(jnp.concatenate(cols, axis=0), tab["bx_i"][...])
        out_ref[0, 4 * g:4 * g + 4] = rows.reshape(4, NY, NX)

    for k in range(SETS):
        drain(s.at[pl.ds(0, 31 * KS)], bsend.at[k])
        drain(p.at[k, :, pl.ds(0, 7 * ZROWS), :], dsend.at[k])
        drain(es.at[k], esend.at[k])
        drain(p.at[k, :, pl.ds(0, 7 * ZROWS), :], fsend.at[k])
    drain(s2.at[pl.ds(0, 31 * ROWS)], hsend)

    @pl.when(tm == L - 1)
    def _():
        drain(sp.at[pl.ds(0, 31 * ROWS)], psend)


def body(iterate, initial):
    dma = pltpu.SemaphoreType.DMA
    vmem = pl.BlockSpec(memory_space=pltpu.VMEM)
    hbm = pl.BlockSpec(memory_space=pl.ANY)
    return pl.pallas_call(
        kernel,
        out_shape=jax.ShapeDtypeStruct(iterate.shape, F32),
        in_specs=[hbm, hbm] + [vmem] * len(NAMES),
        out_specs=vmem,
        scratch_shapes=[
            pltpu.VMEM((PLANES, NY, NX), F32),
            pltpu.VMEM((NY, PLANES, NX), F32),
            pltpu.VMEM((NY, PLANES, NX), F32),
            pltpu.VMEM((SETS, BLOCK, KS, HALF, NX), F32),
            pltpu.VMEM((ROWS, HALF, NX), F32),
            pltpu.VMEM((SETS, BLOCK, KS, HALF, NX), F32),
            pltpu.VMEM((SETS, KS, NZ, NX), F32),
            pltpu.VMEM((SETS, 8, KS, ZROWS, NX), F32),
            pltpu.VMEM((SETS, KS, 2 * BLOCK, NX), F32),
            pltpu.VMEM((SETS, KS, 2 * BLOCK, NX), F32),
            pltpu.VMEM((SETS, KS, 2 * BLOCK, NX), F32),
            pltpu.VMEM((SETS, 4, KS, ZROWS, NX), F32),
            pltpu.VMEM((SETS, KS, NZ, NX), F32),
            pltpu.VMEM((SETS, BLOCK, KS, HALF, NX), F32),
            pltpu.VMEM((NY, PLANES, NX), F32),
            dma, dma, dma((SETS,)), dma((SETS,)), dma, dma, dma((SETS,)), dma((SETS,)),
            dma((SETS,)), dma((SETS,)), dma((SETS,)), dma((SETS,)), dma, dma,
        ],
        compiler_params=pltpu.CompilerParams(
            collective_id=0, has_side_effects=True, vmem_limit_bytes=56 * 1024 * 1024
        ),
        cost_estimate=pl.CostEstimate(flops=4 * 10**9, bytes_accessed=6 * 2**20, transcendentals=0),
        name="paradiag",
    )(iterate, initial, *[jnp.asarray(TABLES[n]) for n in NAMES])


def solution(mesh):
    return jax.shard_map(
        body,
        mesh=mesh,
        in_specs=(P("tm", "gz", None, None), P("gz", None, None)),
        out_specs=P("tm", "gz", None, None),
        check_vma=False,
    )
```

time: 677 us -> 109 us (0.16); the launches traced: 668 us -> 108 us
  waiting for transfers between devices: 225 us -> 0 us
  starting transfers between devices: 134 us -> 0 us
  matrix products: 124 us -> 0 us
  blocking collectives: 123 us -> 0 us
  Pallas kernels: 0 us -> 105 us
  local copies, waits for them, and re-layouts: 52.6 us -> 3.1 us
  other arithmetic: 8.51 us -> 0 us
    all_to_all x8 -> x0, waiting for transfers between devices: 213 us -> none  [the longest x1 42.2 us: body(): lax.all_to_all(spec_im, 'tm', split_axis=0, concat_axis=2, tiled=True)]
    dot_general x28 -> x0, matrix products: 124 us -> none  [apply_table(): return jnp.einsum(FORMS[dim_id], matrix, values, precision=PRECISE)]
    all_to_all x2 -> x0, blocking collectives: 123 us -> none  [the longest x1 67.6 us: body(): lax.all_to_all(source, 'tm', split_axis=2, concat_axis=0, tiled=True)]
    all_to_all x8 -> x0, starting transfers between devices: 120 us -> none  [the longest x1 77.5 us: body(): lax.all_to_all(spec_im, 'tm', split_axis=2, concat_axis=0, tiled=True)]
    pallas_call x0 -> x1, Pallas kernels: none -> 105 us  [body(): pl.pallas_call(kernel, out_shape=jax.ShapeDtypeStruct(iterate.shape, F32)...]
    ppermute x3 -> x0, starting transfers between devices: 14 us -> none  [the longest x1 9.44 us: extended(): lax.ppermute(head, axis, [((i + 1) % count, i) for i in range(count)])]
    all_to_all x8 -> x0, local copies, waits for them, and re-layouts: 12.9 us -> none  [the longest x2 4.31 us: body(): lax.all_to_all(spec_re, 'gz', split_axis=2, concat_axis=1, tiled=True)]
    ppermute x3 -> x0, waiting for transfers between devices: 11.8 us -> none  [the longest x1 8.11 us: extended(): lax.ppermute(tail, axis, [(i, (i + 1) % count) for i in range(count)])]
  transfers between devices with their start and end apart: 11 -> 0, of which waited for: 10 -> 0; matrix products, arithmetic and copies ran while one was open for 13% -> 0% of each run, Pallas kernels for 0% -> 0%
where the time goes in v1:
time: 109 us; the launch traced here: 108 us
  Pallas kernels  105 us (96%)
  local copies, waits for them, and re-layouts  3.1 us (3%)
    pallas_call x1, Pallas kernels, body(): pl.pallas_call(kernel, out_shape=jax.ShapeDtypeStruct(iterate.shape, F32)...  105 us
    unnamed x1, local copies, waits for them, and re-layouts  3.1 us

profile of v1, /device:TPU:1, one launch (start us, length us, event | category | flops | bytes accessed | tf_op | source)
XLA Modules:
  0.0 108.4 jit_solution(17820123956603627940)
XLA Ops:
  0.0 105.3 %paradiag.1 = f32[1,16,128,256]{3,2,1,0:T(8,128)} custom-call(f32[1,16,128,256]{3,2,1,0:T(8,128)} %u_ref.1, f32[16,128,256]{2,1,0:T(8,128)} %init_ref.1, bf16[768,256]{1,0:T(8,128)(2,1)} %constant.28.clone.refs_0_, bf16[768,256]{1,0:T(8,128)(2,1)} %constant.29.clone.refs_1_, bf16[128,384]{1,0:T(8,128)(2,1)} %constant.30.clone.refs_2_, ...), custom_call_target="tpu_custom_call" | custom-call | flops 4000000000 | bytes 6291456 | tf_op jit(solution)/shard_map/paradiag/pallas_call | solution.py:363
  105.3 3.1 %copy.18 = f32[1,16,128,256]{3,2,1,0:T(8,128)} copy(f32[1,16,128,256]{3,2,1,0:T(8,128)} %paradiag.1) | data formatting | bytes 4194304

commit v2 on v1

--- a/solution.py
+++ b/solution.py
@@ -22,7 +22,9 @@
 HALF = NZ // 2
 PLANES = 16
 ROWS = 4
-SETS = 2
+PLACES = 32
+HELP = PLANES // 2
+SETS = 4
 KS = ROWS // SETS
 ZROWS = 16
 
@@ -117,19 +119,28 @@
 
 def kernel(u_ref, init_ref, *refs):
     tab = dict(zip(NAMES, refs[: len(NAMES)]))
-    (out_ref, u, s, sp, r, pb, sq, ys, yr, es, ec, er, fs, p, ws, s2,
-     usem, isem, bsend, brecv, psend, precv, dsend, drecv, esend, erecv, fsend, frecv, hsend, hrecv) = refs[len(NAMES):]
+    (out_ref, u, ty, s, pa, hp, ph, sp, r, pb, sq, ys, yr, es, ec, er, fs, p, ws, s2,
+     usem, isem, osem, bsend, brecv, rsend, rrecv, psend, precv,
+     dsend, drecv, esend, erecv, fsend, frecv, hsend, hrecv) = refs[len(NAMES):]
     tm, gz = lax.axis_index("tm"), lax.axis_index("gz")
     block, step = tm // BLOCK, tm % BLOCK
     half, slab = gz // SLABS, gz % SLABS
     place = step * SLABS + slab
     ring = block * 2 + half
+    last = tm == L - 1
+    helper = jnp.logical_and(step == BLOCK - 1, block % 2 == 0)
+    part = 1 - block // 2
+    origin = jnp.where(block == 0, 1 - half, half)
 
     load = pltpu.make_async_copy(u_ref.at[0], u, usem)
     load.start()
 
+    @pl.when(last)
+    def _():
+        pltpu.make_async_copy(init_ref, pa, isem).start()
+
     def plane_peer(i):
-        t, y = (step + i % BLOCK) % BLOCK, (slab + i // BLOCK) % SLABS
+        t, y = (step + i // SLABS) % BLOCK, (slab + i % SLABS) % SLABS
         return t, y, (block * BLOCK + t, half * SLABS + y)
 
     def ring_peer(i):
@@ -146,71 +157,101 @@
         pl.semaphore_signal(barrier, inc=1, device_id=ring_peer(i)[2], device_id_type=MESH)
         return c
 
-    lax.fori_loop(1, 32, greet_plane, 0)
+    lax.fori_loop(1, PLACES, greet_plane, 0)
     lax.fori_loop(1, 8, greet_ring, 0)
+
+    @pl.when(block == 3)
+    def _():
+        for y in range(SLABS):
+            for dev in ((2 * BLOCK + BLOCK - 1, half * SLABS + y), (BLOCK - 1, (1 - half) * SLABS + y)):
+                pl.semaphore_signal(barrier, inc=1, device_id=dev, device_id_type=MESH)
+
     load.wait()
 
-    def forward(x, dst, z):
-        rows = dot_right(x.reshape(4 * NY, NX), tab["bx_f"][...])
+    def along_y(x, dst, z):
         for i in range(4):
-            dst[:, z + i, :] = dot_left(tab["by_f"][...], rows[i * NY:(i + 1) * NY])
+            dst[:, z + i, :] = dot_left(tab["by_f"][...], x[i])
+
+    def along_x(src, dst, k, planes):
+        rows = src[pl.ds(k * PLACES * KS, PLACES * KS)].reshape(PLACES * KS * planes, NX)
+        dst[pl.ds(k * PLACES * KS, PLACES * KS)] = dot_right(rows, tab["bx_f"][...]).reshape(PLACES * KS, planes, NX)
+
+    @pl.when(last)
+    def _():
+        pltpu.make_async_copy(init_ref, pa, isem).wait()
+        pa[...] = pa[...] * (1.0 / ALPHA) - u[...]
+
+    @pl.when(helper)
+    def _():
+        pl.semaphore_wait(barrier, PLACES - 1 + 7 + PLACES)
+
+    @pl.when(jnp.logical_not(helper))
+    def _():
+        pl.semaphore_wait(barrier, PLACES - 1 + 7)
+
+    def raw(q, c):
+        return pltpu.make_async_remote_copy(
+            src_ref=pa.at[pl.ds(q * HELP + c * 4, 4)], dst_ref=hp.at[pl.ds(c * 4, 4)],
+            send_sem=rsend.at[q, c], recv_sem=rrecv.at[c],
+            device_id=((2 * BLOCK + BLOCK - 1, gz), (BLOCK - 1, (1 - half) * SLABS + slab))[q], device_id_type=MESH,
+        )
+
+    @pl.when(last)
+    def _():
+        for c in range(2):
+            for q in range(2):
+                raw(q, c).start()
 
     for g in range(PLANES // 4):
         x = u[4 * g:4 * g + 4]
-        forward(x * (TIME_STEP * (STABILIZER + 1.0) - TIME_STEP * x * x), s, 4 * g)
-    pl.semaphore_wait(barrier, 38)
+        along_y(x * (TIME_STEP * (STABILIZER + 1.0) - TIME_STEP * x * x), ty, 4 * g)
 
     def send_b(i, c, k):
         t, y, dev = plane_peer(i)
         pltpu.make_async_remote_copy(
-            src_ref=s.at[pl.ds((t * SLABS + y) * ROWS + k * KS, KS)],
+            src_ref=s.at[pl.ds((k * PLACES + t * SLABS + y) * KS, KS)],
             dst_ref=r.at[k, step, :, pl.ds(pl.multiple_of(slab * PLANES, PLANES), PLANES), :],
             send_sem=bsend.at[k], recv_sem=brecv.at[k], device_id=dev, device_id_type=MESH,
         ).start()
         return c
 
+    def send_p(i, c, k):
+        t, y = (step + i // SLABS) % BLOCK, (slab + i % SLABS) % SLABS
+        pltpu.make_async_remote_copy(
+            src_ref=sp.at[pl.ds((k * PLACES + t * SLABS + y) * KS, KS)],
+            dst_ref=pb.at[k, :, pl.ds(pl.multiple_of(slab * PLANES + part * HELP, HELP), HELP), :],
+            send_sem=psend.at[k], recv_sem=precv.at[k], device_id=(3 * BLOCK + t, origin * SLABS + y), device_id_type=MESH,
+        ).start()
+        return c
+
     for k in range(SETS):
-        lax.fori_loop(1, 32, functools.partial(send_b, k=k), 0)
+        along_x(ty, s, k, PLANES)
+        lax.fori_loop(1, PLACES, functools.partial(send_b, k=k), 0)
         pltpu.make_async_copy(
-            s.at[pl.ds(place * ROWS + k * KS, KS)],
+            s.at[pl.ds((k * PLACES + place) * KS, KS)],
             r.at[k, step, :, pl.ds(pl.multiple_of(slab * PLANES, PLANES), PLANES), :],
             brecv.at[k],
         ).start()
 
-    @pl.when(tm == L - 1)
-    def _():
-        load2 = pltpu.make_async_copy(init_ref, out_ref.at[0], isem)
-        load2.start()
-        load2.wait()
-        for g in range(PLANES // 4):
-            forward(out_ref[0, 4 * g:4 * g + 4] * (1.0 / ALPHA) - u[4 * g:4 * g + 4], sp, 4 * g)
-
-        def send_p(i, c):
-            t, y, dev = plane_peer(i)
-            pltpu.make_async_remote_copy(
-                src_ref=sp.at[pl.ds((t * SLABS + y) * ROWS, ROWS)],
-                dst_ref=pb.at[:, pl.ds(pl.multiple_of(slab * PLANES, PLANES), PLANES), :],
-                send_sem=psend, recv_sem=precv, device_id=dev, device_id_type=MESH,
-            ).start()
-            return c
-
-        lax.fori_loop(1, 32, send_p, 0)
-        pltpu.make_async_copy(
-            sp.at[pl.ds(place * ROWS, ROWS)],
-            pb.at[:, pl.ds(pl.multiple_of(slab * PLANES, PLANES), PLANES), :],
-            precv,
-        ).start()
+        @pl.when(helper)
+        def _():
+            if k == 0:
+                for c in range(2):
+                    drain(hp.at[pl.ds(c * 4, 4)], rrecv.at[c])
+                    along_y(hp[4 * c:4 * c + 4], ph, 4 * c)
+            along_x(ph, sp, k, HELP)
+            lax.fori_loop(0, PLACES, functools.partial(send_p, k=k), 0)
 
     def decay(k, j, table):
-        row = tab["lxy"][pl.ds(place * ROWS + k * KS + j, 1), :]
+        row = tab["lxy"][pl.ds((k * PLACES + place) * KS + j, 1), :]
         return 1.0 / (row + twice(table))
 
     def stage_c(k):
         drain(r.at[k], brecv.at[k])
-        if k == 0:
-            @pl.when(block == 3)
-            def _():
-                drain(pb, precv)
+
+        @pl.when(block == 3)
+        def _():
+            drain(pb.at[k], precv.at[k])
 
         def one(j, c):
             a = decay(k, j, tab["lz"][...])
@@ -234,7 +275,7 @@
         @pl.when(block == 3)
         def _():
             def add(j, c):
-                ys[k, j] += dot_left(tab["bz_f"][...], pb[k * KS + j])
+                ys[k, j] += dot_left(tab["bz_f"][...], pb[k, j])
                 return c
             lax.fori_loop(0, KS, add, 0)
 
@@ -319,30 +360,38 @@
             t, y, dev = plane_peer(i)
             pltpu.make_async_remote_copy(
                 src_ref=ws.at[k, t, :, pl.ds(pl.multiple_of(y * PLANES, PLANES), PLANES), :],
-                dst_ref=s2.at[pl.ds(place * ROWS + k * KS, KS)],
-                send_sem=hsend, recv_sem=hrecv, device_id=dev, device_id_type=MESH,
+                dst_ref=s2.at[pl.ds((k * PLACES + place) * KS, KS)],
+                send_sem=hsend, recv_sem=hrecv.at[k], device_id=dev, device_id_type=MESH,
             ).start()
             return c
 
         lax.fori_loop(1, 32, send_h, 0)
         pltpu.make_async_copy(
             ws.at[k, step, :, pl.ds(pl.multiple_of(slab * PLANES, PLANES), PLANES), :],
-            s2.at[pl.ds(place * ROWS + k * KS, KS)],
-            hrecv,
-        ).start()
-
-    if SETS == 1:
-        order = [(stage_c, 0), (stage_e, 0), (stage_g, 0)]
-    else:
-        order = [(stage_c, 0), (stage_e, 0), (stage_c, 1), (stage_g, 0), (stage_e, 1), (stage_g, 1)]
-    for stage, k in order:
-        stage(k)
-
-    drain(s2, hrecv)
+            s2.at[pl.ds((k * PLACES + place) * KS, KS)],
+            hrecv.at[k],
+        ).start()
+
+    for k in range(SETS):
+        stage_c(k)
+        if k > 0:
+            stage_g(k - 1)
+        stage_e(k)
+    stage_g(SETS - 1)
+
+    for k in range(SETS):
+        rows = pl.ds(k * PLACES * KS, PLACES * KS)
+        drain(s2.at[rows], hrecv.at[k])
+        x = dot_right(s2[rows].reshape(PLACES * KS * PLANES, NX), tab["bx_i"][...])
+        ty[rows] = x.reshape(PLACES * KS, PLANES, NX)
+
+    def store(g):
+        return pltpu.make_async_copy(u.at[pl.ds(4 * g, 4)], out_ref.at[0, pl.ds(4 * g, 4)], osem.at[g])
+
     for g in range(PLANES // 4):
-        cols = [dot_left(tab["by_i"][...], s2[:, 4 * g + i, :]) for i in range(4)]
-        rows = dot_right(jnp.concatenate(cols, axis=0), tab["bx_i"][...])
-        out_ref[0, 4 * g:4 * g + 4] = rows.reshape(4, NY, NX)
+        for i in range(4):
+            u[4 * g + i] = dot_left(tab["by_i"][...], ty[:, 4 * g + i, :])
+        store(g).start()
 
     for k in range(SETS):
         drain(s.at[pl.ds(0, 31 * KS)], bsend.at[k])
@@ -351,9 +400,19 @@
         drain(p.at[k, :, pl.ds(0, 7 * ZROWS), :], fsend.at[k])
     drain(s2.at[pl.ds(0, 31 * ROWS)], hsend)
 
-    @pl.when(tm == L - 1)
-    def _():
-        drain(sp.at[pl.ds(0, 31 * ROWS)], psend)
+    @pl.when(last)
+    def _():
+        for c in range(2):
+            for q in range(2):
+                drain(pa.at[pl.ds(0, 4)], rsend.at[q, c])
+
+    @pl.when(helper)
+    def _():
+        for k in range(SETS):
+            drain(sp.at[pl.ds(0, PLACES * KS)], psend.at[k])
+
+    for g in range(PLANES // 4):
+        store(g).wait()
 
 
 def body(iterate, initial):
@@ -364,13 +423,17 @@
         kernel,
         out_shape=jax.ShapeDtypeStruct(iterate.shape, F32),
         in_specs=[hbm, hbm] + [vmem] * len(NAMES),
-        out_specs=vmem,
+        out_specs=hbm,
         scratch_shapes=[
             pltpu.VMEM((PLANES, NY, NX), F32),
             pltpu.VMEM((NY, PLANES, NX), F32),
             pltpu.VMEM((NY, PLANES, NX), F32),
+            pltpu.VMEM((PLANES, NY, NX), F32),
+            pltpu.VMEM((HELP, NY, NX), F32),
+            pltpu.VMEM((NY, HELP, NX), F32),
+            pltpu.VMEM((NY, HELP, NX), F32),
             pltpu.VMEM((SETS, BLOCK, KS, HALF, NX), F32),
-            pltpu.VMEM((ROWS, HALF, NX), F32),
+            pltpu.VMEM((SETS, KS, HALF, NX), F32),
             pltpu.VMEM((SETS, BLOCK, KS, HALF, NX), F32),
             pltpu.VMEM((SETS, KS, NZ, NX), F32),
             pltpu.VMEM((SETS, 8, KS, ZROWS, NX), F32),
@@ -381,8 +444,10 @@
             pltpu.VMEM((SETS, KS, NZ, NX), F32),
             pltpu.VMEM((SETS, BLOCK, KS, HALF, NX), F32),
             pltpu.VMEM((NY, PLANES, NX), F32),
-            dma, dma, dma((SETS,)), dma((SETS,)), dma, dma, dma((SETS,)), dma((SETS,)),
-            dma((SETS,)), dma((SETS,)), dma((SETS,)), dma((SETS,)), dma, dma,
+            dma, dma, dma((PLANES // 4,)),
+            dma((SETS,)), dma((SETS,)), dma((2, 2)), dma((2,)), dma((SETS,)), dma((SETS,)),
+            dma((SETS,)), dma((SETS,)), dma((SETS,)), dma((SETS,)), dma((SETS,)), dma((SETS,)),
+            dma, dma((SETS,)),
         ],
         compiler_params=pltpu.CompilerParams(
             collective_id=0, has_side_effects=True, vmem_limit_bytes=56 * 1024 * 1024

time: 109 us -> 93.7 us (0.86)
  Pallas kernels: 105 us -> 90.4 us
    pallas_call x1, Pallas kernels: 105 us -> 90.4 us  [body(): pl.pallas_call(kernel, out_shape=jax.ShapeDtypeStruct(iterate.shape, F32)...]
where the time goes in v2:
time: 93.7 us; the launch traced here: 93.5 us
  Pallas kernels  90.4 us (96%)
  local copies, waits for them, and re-layouts  3.1 us (3%)
    pallas_call x1, Pallas kernels, body(): pl.pallas_call(kernel, out_shape=jax.ShapeDtypeStruct(iterate.shape, F32)...  90.4 us
    unnamed x1, local copies, waits for them, and re-layouts  3.1 us

profile of v2, /device:TPU:1, one launch (start us, length us, event | category | flops | bytes accessed | tf_op | source)
XLA Modules:
  0.0 93.5 jit_solution(5436638850937274466)
XLA Ops:
  0.0 90.4 %paradiag.1 = f32[1,16,128,256]{3,2,1,0:T(8,128)} custom-call(f32[1,16,128,256]{3,2,1,0:T(8,128)} %u_ref.1, f32[16,128,256]{2,1,0:T(8,128)} %init_ref.1, bf16[768,256]{1,0:T(8,128)(2,1)} %constant.28.clone.refs_0_, bf16[768,256]{1,0:T(8,128)(2,1)} %constant.29.clone.refs_1_, bf16[128,384]{1,0:T(8,128)(2,1)} %constant.30.clone.refs_2_, ...), custom_call_target="tpu_custom_call" | custom-call | flops 4000000000 | bytes 6291456 | tf_op jit(solution)/shard_map/paradiag/pallas_call | solution.py:422
  90.4 3.1 %copy.18 = f32[1,16,128,256]{3,2,1,0:T(8,128)} copy(f32[1,16,128,256]{3,2,1,0:T(8,128)} %paradiag.1) | data formatting | bytes 4194304

commit v3 on v2

--- a/solution.py
+++ b/solution.py
@@ -23,10 +23,25 @@
 PLANES = 16
 ROWS = 4
 PLACES = 32
-HELP = PLANES // 2
+HELP = 2
+HELP_AFTER = 0
 SETS = 4
 KS = ROWS // SETS
 ZROWS = 16
+
+
+def peers():
+    found = []
+    for x in range(4):
+        for core in range(2):
+            for y in range(SLABS):
+                for one in ((x, core, y), (-x % 4, core, -y % SLABS)):
+                    if one not in found and one != (0, 0, 0):
+                        found.append(one)
+    return found
+
+
+PEERS = peers()
 
 
 def real_basis(n):
@@ -74,7 +89,7 @@
         bx_i=right(bx),
         by_i=left(by.T),
         bz_s=left(np.concatenate([bz[:, :HALF], sine], axis=0)),
-        bz_f=left(bz[:, :HALF]),
+        bz_p=left(bz[:, [i + HELP * n for i in range(HELP) for n in range(HALF // HELP)]]),
         bz_i=left(sine @ bz[:, :HALF].T),
         sine=left(sine),
         lxy=(base + COUPLING * (ly[:, None] + lx[None, :])).astype(np.float32),
@@ -119,7 +134,7 @@
 
 def kernel(u_ref, init_ref, *refs):
     tab = dict(zip(NAMES, refs[: len(NAMES)]))
-    (out_ref, u, ty, s, pa, hp, ph, sp, r, pb, sq, ys, yr, es, ec, er, fs, p, ws, s2,
+    (out_ref, u, ty, s, pa, hp, sp, r, pb, sq, ys, yr, es, ec, er, fs, p, ws, s2,
      usem, isem, osem, bsend, brecv, rsend, rrecv, psend, precv,
      dsend, drecv, esend, erecv, fsend, frecv, hsend, hrecv) = refs[len(NAMES):]
     tm, gz = lax.axis_index("tm"), lax.axis_index("gz")
@@ -127,20 +142,25 @@
     half, slab = gz // SLABS, gz % SLABS
     place = step * SLABS + slab
     ring = block * 2 + half
+    x, core = step // 2, step % 2
     last = tm == L - 1
-    helper = jnp.logical_and(step == BLOCK - 1, block % 2 == 0)
-    part = 1 - block // 2
-    origin = jnp.where(block == 0, 1 - half, half)
+    beside = jnp.logical_and(block == 3, jnp.logical_or(x % 2 == 0, step == BLOCK - 2))
+    above = jnp.logical_and(x == 3, jnp.logical_or(block == 2, jnp.logical_and(block == 1, core == 0)))
+    helper = jnp.logical_or(beside, above)
+    part = jnp.where(block == 3, jnp.where(x == 3, 4, x + core), jnp.where(block == 2, 5 + core, 7))
 
     load = pltpu.make_async_copy(u_ref.at[0], u, usem)
     load.start()
 
-    @pl.when(last)
-    def _():
-        pltpu.make_async_copy(init_ref, pa, isem).start()
-
-    def plane_peer(i):
-        t, y = (step + i // SLABS) % BLOCK, (slab + i % SLABS) % SLABS
+    state = pltpu.make_async_copy(init_ref.at[pl.ds(part * HELP, HELP)], pa, isem)
+
+    @pl.when(helper)
+    def _():
+        state.start()
+
+    def plane_peer(one):
+        dx, dc, dy = one
+        t, y = (x + dx) % 4 * 2 + (core + dc) % 2, (slab + dy) % SLABS
         return t, y, (block * BLOCK + t, half * SLABS + y)
 
     def ring_peer(i):
@@ -149,98 +169,113 @@
 
     barrier = pltpu.get_barrier_semaphore()
 
-    def greet_plane(i, c):
-        pl.semaphore_signal(barrier, inc=1, device_id=plane_peer(i)[2], device_id_type=MESH)
-        return c
-
-    def greet_ring(i, c):
-        pl.semaphore_signal(barrier, inc=1, device_id=ring_peer(i)[2], device_id_type=MESH)
-        return c
-
-    lax.fori_loop(1, PLACES, greet_plane, 0)
-    lax.fori_loop(1, 8, greet_ring, 0)
+    def greet(dev):
+        pl.semaphore_signal(barrier, inc=1, device_id=dev, device_id_type=MESH)
+
+    for one in PEERS:
+        greet(plane_peer(one)[2])
+    for i in range(1, 8):
+        greet(ring_peer(i)[2])
 
     @pl.when(block == 3)
     def _():
         for y in range(SLABS):
-            for dev in ((2 * BLOCK + BLOCK - 1, half * SLABS + y), (BLOCK - 1, (1 - half) * SLABS + y)):
-                pl.semaphore_signal(barrier, inc=1, device_id=dev, device_id_type=MESH)
+            for c in range(2):
+                greet((2 * BLOCK + 6 + c, half * SLABS + y))
+            greet((BLOCK + 6, half * SLABS + y))
+
+    @pl.when(jnp.logical_and(above, core == 0))
+    def _():
+        greet((L - 1, gz))
+
+    greeted = PLACES - 1 + 7
+
+    @pl.when(last)
+    def _():
+        pl.semaphore_wait(barrier, greeted + 2)
 
     load.wait()
+
+    @pl.when(last)
+    def _():
+        for c in range(4 * HELP):
+            for q in (0, 2, 5, 4, 1, 3, 6, 7):
+                where = (pl.ds(c // 4, 1), pl.ds(c % 4 * 32, 32))
+                pltpu.make_async_remote_copy(
+                    src_ref=u.at[pl.ds(q * HELP + c // 4, 1), where[1]], dst_ref=hp.at[where],
+                    send_sem=rsend, recv_sem=rrecv,
+                    device_id=((24, 25, 28, 29, 30, 22, 23, 14)[q], gz), device_id_type=MESH,
+                ).start()
+
 
     def along_y(x, dst, z):
         for i in range(4):
             dst[:, z + i, :] = dot_left(tab["by_f"][...], x[i])
 
-    def along_x(src, dst, k, planes):
-        rows = src[pl.ds(k * PLACES * KS, PLACES * KS)].reshape(PLACES * KS * planes, NX)
-        dst[pl.ds(k * PLACES * KS, PLACES * KS)] = dot_right(rows, tab["bx_f"][...]).reshape(PLACES * KS, planes, NX)
-
-    @pl.when(last)
-    def _():
-        pltpu.make_async_copy(init_ref, pa, isem).wait()
-        pa[...] = pa[...] * (1.0 / ALPHA) - u[...]
-
-    @pl.when(helper)
-    def _():
-        pl.semaphore_wait(barrier, PLACES - 1 + 7 + PLACES)
-
-    @pl.when(jnp.logical_not(helper))
-    def _():
-        pl.semaphore_wait(barrier, PLACES - 1 + 7)
-
-    def raw(q, c):
-        return pltpu.make_async_remote_copy(
-            src_ref=pa.at[pl.ds(q * HELP + c * 4, 4)], dst_ref=hp.at[pl.ds(c * 4, 4)],
-            send_sem=rsend.at[q, c], recv_sem=rrecv.at[c],
-            device_id=((2 * BLOCK + BLOCK - 1, gz), (BLOCK - 1, (1 - half) * SLABS + slab))[q], device_id_type=MESH,
-        )
-
-    @pl.when(last)
-    def _():
-        for c in range(2):
-            for q in range(2):
-                raw(q, c).start()
+    def along_x(k):
+        rows = pl.ds(k * PLACES * KS, PLACES * KS)
+        done = dot_right(ty[rows].reshape(PLACES * KS * PLANES, NX), tab["bx_f"][...])
+        s[rows] = done.reshape(PLACES * KS, PLANES, NX)
 
     for g in range(PLANES // 4):
-        x = u[4 * g:4 * g + 4]
-        along_y(x * (TIME_STEP * (STABILIZER + 1.0) - TIME_STEP * x * x), ty, 4 * g)
-
-    def send_b(i, c, k):
-        t, y, dev = plane_peer(i)
+        v = u[4 * g:4 * g + 4]
+        along_y(v * (TIME_STEP * (STABILIZER + 1.0) - TIME_STEP * v * v), ty, 4 * g)
+
+    @pl.when(above)
+    def _():
+        pl.semaphore_wait(barrier, greeted + PLACES)
+
+    @pl.when(jnp.logical_not(jnp.logical_or(above, last)))
+    def _():
+        pl.semaphore_wait(barrier, greeted)
+
+    def send_b(one, k):
+        t, y, dev = plane_peer(one)
         pltpu.make_async_remote_copy(
             src_ref=s.at[pl.ds((k * PLACES + t * SLABS + y) * KS, KS)],
             dst_ref=r.at[k, step, :, pl.ds(pl.multiple_of(slab * PLANES, PLANES), PLANES), :],
             send_sem=bsend.at[k], recv_sem=brecv.at[k], device_id=dev, device_id_type=MESH,
         ).start()
-        return c
-
-    def send_p(i, c, k):
-        t, y = (step + i // SLABS) % BLOCK, (slab + i % SLABS) % SLABS
+
+    def send_p(one):
+        t, y, _ = plane_peer(one)
         pltpu.make_async_remote_copy(
-            src_ref=sp.at[pl.ds((k * PLACES + t * SLABS + y) * KS, KS)],
-            dst_ref=pb.at[k, :, pl.ds(pl.multiple_of(slab * PLANES + part * HELP, HELP), HELP), :],
-            send_sem=psend.at[k], recv_sem=precv.at[k], device_id=(3 * BLOCK + t, origin * SLABS + y), device_id_type=MESH,
-        ).start()
-        return c
+            src_ref=sp.at[t * SLABS + y], dst_ref=pb.at[slab * 8 + part],
+            send_sem=psend, recv_sem=precv, device_id=(3 * BLOCK + t, half * SLABS + y), device_id_type=MESH,
+        ).start()
 
     for k in range(SETS):
-        along_x(ty, s, k, PLANES)
-        lax.fori_loop(1, PLACES, functools.partial(send_b, k=k), 0)
+        along_x(k)
+        for one in PEERS:
+            send_b(one, k)
         pltpu.make_async_copy(
             s.at[pl.ds((k * PLACES + place) * KS, KS)],
             r.at[k, step, :, pl.ds(pl.multiple_of(slab * PLANES, PLANES), PLANES), :],
             brecv.at[k],
         ).start()
+        if k != HELP_AFTER:
+            continue
+
 
         @pl.when(helper)
         def _():
-            if k == 0:
-                for c in range(2):
-                    drain(hp.at[pl.ds(c * 4, 4)], rrecv.at[c])
-                    along_y(hp[4 * c:4 * c + 4], ph, 4 * c)
-            along_x(ph, sp, k, HELP)
-            lax.fori_loop(0, PLACES, functools.partial(send_p, k=k), 0)
+            state.wait()
+            drain(hp, rrecv)
+            rows = [dot_left(tab["by_f"][...], pa[i] * (1.0 / ALPHA) - hp[i]) for i in range(HELP)]
+            rows = dot_right(jnp.concatenate(rows, axis=0), tab["bx_f"][...])
+            for i in range(HELP):
+                for m in range(ROWS):
+                    sp[:, HELP * m + i, :] = rows[i * NY + m * PLACES:i * NY + (m + 1) * PLACES]
+            for one in PEERS:
+                send_p(one)
+
+        @pl.when(beside)
+        def _():
+            pltpu.make_async_copy(sp.at[place], pb.at[slab * 8 + part], precv).start()
+
+        @pl.when(above)
+        def _():
+            send_p((0, 0, 0))
 
     def decay(k, j, table):
         row = tab["lxy"][pl.ds((k * PLACES + place) * KS + j, 1), :]
@@ -249,9 +284,10 @@
     def stage_c(k):
         drain(r.at[k], brecv.at[k])
 
-        @pl.when(block == 3)
-        def _():
-            drain(pb.at[k], precv.at[k])
+        if k == 0:
+            @pl.when(block == 3)
+            def _():
+                drain(pb, precv)
 
         def one(j, c):
             a = decay(k, j, tab["lz"][...])
@@ -275,20 +311,21 @@
         @pl.when(block == 3)
         def _():
             def add(j, c):
-                ys[k, j] += dot_left(tab["bz_f"][...], pb[k, j])
+                extra = [pb[:, HELP * k + i, :] for i in range(HELP)]
+                ys[k, j] += dot_left(tab["bz_p"][...], jnp.concatenate(extra, axis=0))
                 return c
             lax.fori_loop(0, KS, add, 0)
 
-        def send_d(i, c):
+        def send_d(i):
             to_b, to_h, dev = ring_peer(i)
             pltpu.make_async_remote_copy(
                 src_ref=ys.at[k, :, pl.ds(pl.multiple_of((to_b * 2 + to_h) * ZROWS, ZROWS), ZROWS), :],
                 dst_ref=yr.at[k, ring],
                 send_sem=dsend.at[k], recv_sem=drecv.at[k], device_id=dev, device_id_type=MESH,
             ).start()
-            return c
-
-        lax.fori_loop(1, 8, send_d, 0)
+
+        for i in range(1, 8):
+            send_d(i)
         pltpu.make_async_copy(
             ys.at[k, :, pl.ds(pl.multiple_of(ring * ZROWS, ZROWS), ZROWS), :], yr.at[k, ring], drecv.at[k]
         ).start()
@@ -317,16 +354,16 @@
                 fs[k, b, j] = prev
                 prev = ends[b] + g * prev
 
-        def send_f(i, c):
+        def send_f(i):
             to_b, to_h, dev = ring_peer(i)
             pltpu.make_async_remote_copy(
                 src_ref=fs.at[k, to_b],
                 dst_ref=p.at[k, :, pl.ds(pl.multiple_of(ring * ZROWS, ZROWS), ZROWS), :],
                 send_sem=fsend.at[k], recv_sem=frecv.at[k], device_id=dev, device_id_type=MESH,
             ).start()
-            return c
-
-        lax.fori_loop(1, 8, send_f, 0)
+
+        for i in range(1, 8):
+            send_f(i)
         pltpu.make_async_copy(
             fs.at[k, block], p.at[k, :, pl.ds(pl.multiple_of(ring * ZROWS, ZROWS), ZROWS), :], frecv.at[k]
         ).start()
@@ -356,16 +393,16 @@
 
         lax.fori_loop(0, KS, one, 0)
 
-        def send_h(i, c):
-            t, y, dev = plane_peer(i)
+        def send_h(one):
+            t, y, dev = plane_peer(one)
             pltpu.make_async_remote_copy(
                 src_ref=ws.at[k, t, :, pl.ds(pl.multiple_of(y * PLANES, PLANES), PLANES), :],
                 dst_ref=s2.at[pl.ds((k * PLACES + place) * KS, KS)],
                 send_sem=hsend, recv_sem=hrecv.at[k], device_id=dev, device_id_type=MESH,
             ).start()
-            return c
-
-        lax.fori_loop(1, 32, send_h, 0)
+
+        for one in PEERS:
+            send_h(one)
         pltpu.make_async_copy(
             ws.at[k, step, :, pl.ds(pl.multiple_of(slab * PLANES, PLANES), PLANES), :],
             s2.at[pl.ds((k * PLACES + place) * KS, KS)],
@@ -375,15 +412,22 @@
     for k in range(SETS):
         stage_c(k)
         if k > 0:
-            stage_g(k - 1)
-        stage_e(k)
+            stage_e(k - 1)
+        if k > 1:
+            stage_g(k - 2)
+    stage_e(SETS - 1)
+    stage_g(SETS - 2)
     stage_g(SETS - 1)
 
     for k in range(SETS):
         rows = pl.ds(k * PLACES * KS, PLACES * KS)
         drain(s2.at[rows], hrecv.at[k])
-        x = dot_right(s2[rows].reshape(PLACES * KS * PLANES, NX), tab["bx_i"][...])
-        ty[rows] = x.reshape(PLACES * KS, PLANES, NX)
+        back = dot_right(s2[rows].reshape(PLACES * KS * PLANES, NX), tab["bx_i"][...])
+        ty[rows] = back.reshape(PLACES * KS, PLANES, NX)
+
+    @pl.when(last)
+    def _():
+        drain(u, rsend)
 
     def store(g):
         return pltpu.make_async_copy(u.at[pl.ds(4 * g, 4)], out_ref.at[0, pl.ds(4 * g, 4)], osem.at[g])
@@ -400,16 +444,13 @@
         drain(p.at[k, :, pl.ds(0, 7 * ZROWS), :], fsend.at[k])
     drain(s2.at[pl.ds(0, 31 * ROWS)], hsend)
 
-    @pl.when(last)
-    def _():
-        for c in range(2):
-            for q in range(2):
-                drain(pa.at[pl.ds(0, 4)], rsend.at[q, c])
-
     @pl.when(helper)
     def _():
-        for k in range(SETS):
-            drain(sp.at[pl.ds(0, PLACES * KS)], psend.at[k])
+        drain(sp.at[pl.ds(0, PLACES - 1)], psend)
+
+    @pl.when(above)
+    def _():
+        drain(sp.at[0], psend)
 
     for g in range(PLANES // 4):
         store(g).wait()
@@ -428,12 +469,11 @@
             pltpu.VMEM((PLANES, NY, NX), F32),
             pltpu.VMEM((NY, PLANES, NX), F32),
             pltpu.VMEM((NY, PLANES, NX), F32),
-            pltpu.VMEM((PLANES, NY, NX), F32),
             pltpu.VMEM((HELP, NY, NX), F32),
-            pltpu.VMEM((NY, HELP, NX), F32),
-            pltpu.VMEM((NY, HELP, NX), F32),
+            pltpu.VMEM((HELP, NY, NX), F32),
+            pltpu.VMEM((PLACES, HELP * ROWS, NX), F32),
             pltpu.VMEM((SETS, BLOCK, KS, HALF, NX), F32),
-            pltpu.VMEM((SETS, KS, HALF, NX), F32),
+            pltpu.VMEM((PLACES, HELP * ROWS, NX), F32),
             pltpu.VMEM((SETS, BLOCK, KS, HALF, NX), F32),
             pltpu.VMEM((SETS, KS, NZ, NX), F32),
             pltpu.VMEM((SETS, 8, KS, ZROWS, NX), F32),
@@ -445,7 +485,7 @@
             pltpu.VMEM((SETS, BLOCK, KS, HALF, NX), F32),
             pltpu.VMEM((NY, PLANES, NX), F32),
             dma, dma, dma((PLANES // 4,)),
-            dma((SETS,)), dma((SETS,)), dma((2, 2)), dma((2,)), dma((SETS,)), dma((SETS,)),
+            dma((SETS,)), dma((SETS,)), dma, dma, dma, dma,
             dma((SETS,)), dma((SETS,)), dma((SETS,)), dma((SETS,)), dma((SETS,)), dma((SETS,)),
             dma, dma((SETS,)),
         ],

time: 93.7 us -> 86.3 us (0.921)
  Pallas kernels: 90.4 us -> 83.1 us
    pallas_call x1, Pallas kernels: 90.4 us -> 83.1 us  [body(): pl.pallas_call(kernel, out_shape=jax.ShapeDtypeStruct(iterate.shape, F32)...]
where the time goes in v3:
time: 86.3 us; the launch traced here: 86.2 us
  Pallas kernels  83.1 us (96%)
  local copies, waits for them, and re-layouts  3.1 us (4%)
    pallas_call x1, Pallas kernels, body(): pl.pallas_call(kernel, out_shape=jax.ShapeDtypeStruct(iterate.shape, F32)...  83.1 us
    unnamed x1, local copies, waits for them, and re-layouts  3.1 us

profile of v3, /device:TPU:1, one launch (start us, length us, event | category | flops | bytes accessed | tf_op | source)
XLA Modules:
  0.0 86.2 jit_solution(1868890443681754622)
XLA Ops:
  0.0 83.1 %paradiag.1 = f32[1,16,128,256]{3,2,1,0:T(8,128)} custom-call(f32[1,16,128,256]{3,2,1,0:T(8,128)} %u_ref.1, f32[16,128,256]{2,1,0:T(8,128)} %init_ref.1, bf16[768,256]{1,0:T(8,128)(2,1)} %constant.28.clone.refs_0_, bf16[768,256]{1,0:T(8,128)(2,1)} %constant.29.clone.refs_1_, bf16[128,384]{1,0:T(8,128)(2,1)} %constant.30.clone.refs_2_, ...), custom_call_target="tpu_custom_call" | custom-call | flops 4000000000 | bytes 6291456 | tf_op jit(solution)/shard_map/paradiag/pallas_call | solution.py:463
  83.1 3.1 %copy.18 = f32[1,16,128,256]{3,2,1,0:T(8,128)} copy(f32[1,16,128,256]{3,2,1,0:T(8,128)} %paradiag.1) | data formatting | bytes 4194304

commit v4 on v3

--- a/solution.py
+++ b/solution.py
@@ -32,12 +32,12 @@
 
 def peers():
     found = []
-    for x in range(4):
-        for core in range(2):
-            for y in range(SLABS):
-                for one in ((x, core, y), (-x % 4, core, -y % SLABS)):
-                    if one not in found and one != (0, 0, 0):
-                        found.append(one)
+    every = [(x, core, y) for x in range(4) for core in range(2) for y in range(SLABS)]
+    every.sort(key=lambda one: -min(one[0], 4 - one[0]) - min(one[2], 4 - one[2]))
+    for x, core, y in every:
+        for one in ((x, core, y), (y, core, x), (-x % 4, core, -y % 4), (-y % 4, core, -x % 4)):
+            if one not in found and one != (0, 0, 0):
+                found.append(one)
     return found
 
 

time: 86.3 us -> 86.5 us (level)
  no operation moved by 1% of the time
where the time goes in v4:
time: 86.5 us; the launch traced here: 86.3 us
  Pallas kernels  83.2 us (96%)
  local copies, waits for them, and re-layouts  3.1 us (4%)
    pallas_call x1, Pallas kernels, body(): pl.pallas_call(kernel, out_shape=jax.ShapeDtypeStruct(iterate.shape, F32)...  83.2 us
    unnamed x1, local copies, waits for them, and re-layouts  3.1 us

profile of v4, /device:TPU:1, one launch (start us, length us, event | category | flops | bytes accessed | tf_op | source)
XLA Modules:
  0.0 86.3 jit_solution(2864450793305849425)
XLA Ops:
  0.0 83.2 %paradiag.1 = f32[1,16,128,256]{3,2,1,0:T(8,128)} custom-call(f32[1,16,128,256]{3,2,1,0:T(8,128)} %u_ref.1, f32[16,128,256]{2,1,0:T(8,128)} %init_ref.1, bf16[768,256]{1,0:T(8,128)(2,1)} %constant.28.clone.refs_0_, bf16[768,256]{1,0:T(8,128)(2,1)} %constant.29.clone.refs_1_, bf16[128,384]{1,0:T(8,128)(2,1)} %constant.30.clone.refs_2_, ...), custom_call_target="tpu_custom_call" | custom-call | flops 4000000000 | bytes 6291456 | tf_op jit(solution)/shard_map/paradiag/pallas_call | solution.py:463
  83.2 3.1 %copy.18 = f32[1,16,128,256]{3,2,1,0:T(8,128)} copy(f32[1,16,128,256]{3,2,1,0:T(8,128)} %paradiag.1) | data formatting | bytes 4194304

commit v5 on v3

--- a/solution.py
+++ b/solution.py
@@ -199,7 +199,7 @@
     @pl.when(last)
     def _():
         for c in range(4 * HELP):
-            for q in (0, 2, 5, 4, 1, 3, 6, 7):
+            for q in (5, 0, 2, 6, 1, 3, 7, 4):
                 where = (pl.ds(c // 4, 1), pl.ds(c % 4 * 32, 32))
                 pltpu.make_async_remote_copy(
                     src_ref=u.at[pl.ds(q * HELP + c // 4, 1), where[1]], dst_ref=hp.at[where],

time: 86.3 us -> 86.5 us (level)
  no operation moved by 1% of the time
where the time goes in v5:
time: 86.5 us; the launch traced here: 86.4 us
  Pallas kernels  83.3 us (96%)
  local copies, waits for them, and re-layouts  3.1 us (4%)
    pallas_call x1, Pallas kernels, body(): pl.pallas_call(kernel, out_shape=jax.ShapeDtypeStruct(iterate.shape, F32)...  83.3 us
    unnamed x1, local copies, waits for them, and re-layouts  3.1 us

profile of v5, /device:TPU:1, one launch (start us, length us, event | category | flops | bytes accessed | tf_op | source)
XLA Modules:
  0.0 86.4 jit_solution(984114033482678390)
XLA Ops:
  0.0 83.3 %paradiag.1 = f32[1,16,128,256]{3,2,1,0:T(8,128)} custom-call(f32[1,16,128,256]{3,2,1,0:T(8,128)} %u_ref.1, f32[16,128,256]{2,1,0:T(8,128)} %init_ref.1, bf16[768,256]{1,0:T(8,128)(2,1)} %constant.28.clone.refs_0_, bf16[768,256]{1,0:T(8,128)(2,1)} %constant.29.clone.refs_1_, bf16[128,384]{1,0:T(8,128)(2,1)} %constant.30.clone.refs_2_, ...), custom_call_target="tpu_custom_call" | custom-call | flops 4000000000 | bytes 6291456 | tf_op jit(solution)/shard_map/paradiag/pallas_call | solution.py:463
  83.3 3.1 %copy.18 = f32[1,16,128,256]{3,2,1,0:T(8,128)} copy(f32[1,16,128,256]{3,2,1,0:T(8,128)} %paradiag.1) | data formatting | bytes 4194304
